TPU v7x, 32 devices: a whole 2x2x4 slice. The times are simulated.
32 devices in a mesh: rows: 4 (over y, core), acts: 8 (over z, x).
Axes of the slice: x: 2, y: 2, z: 4, core: 2. Of those that a mesh axis runs over, the one named last changes fastest.
Arguments:
- features: bfloat16 [16384, 2048], P('rows'), may hold values from -6 to 80
- policy_weight: bfloat16 [2048, 4096], P(None, 'acts'), may hold values from -3 to 3
- reward_weight: bfloat16 [2048, 4096], P(None, 'acts'), may hold values from -1 to 1
- logged_action: int32 [16384], P('rows'), may hold values from 0 to 4095
- reward_level: int32 [16384], P('rows'), may hold values from 0 to 4
- logged_propensity: float32 [16384], P('rows'), may hold values from 9.765625e-05 to 0.0009765625
Outputs:
- policy_grad: float32 [2048, 4096], P(None, 'acts')
- reward_grad: float32 [2048, 4096], P(None, 'acts')
- row_value: float32 [16384], P('rows')
All inputs are finite; a program needn't handle non-finite values.
Results may differ from a plain program's by a relative error of at most 0.015.
Values may be sent and summed in bfloat16 or wider, within the bound.
A program may use at most 128 MiB of HBM per device.

v0:
```python
import jax
import jax.numpy as jnp
from jax import lax
from jax.sharding import PartitionSpec as P


def finish_rows(
    exponent, row_total, weighted, picked_exp, picked_pred, predicted, onehot, payoff, propensity
):
    probability = exponent / row_total[:, None]
    mean_pred = weighted / row_total
    importance = picked_exp / row_total / propensity
    corrected = importance * (payoff - picked_pred)
    row_value = mean_pred + corrected
    policy_term = (
        probability * (predicted - mean_pred[:, None])
        + corrected[:, None] * (onehot.astype(jnp.float32) - probability)
    ).astype(jnp.bfloat16)
    reward_term = jnp.where(onehot, predicted - payoff[:, None], jnp.float32(0.0)).astype(
        jnp.bfloat16
    )
    return (policy_term, reward_term, row_value)


def on_device(
    features, policy_weight, reward_weight, logged_action, reward_level, logged_propensity
):
    scores = jnp.dot(features, policy_weight, preferred_element_type=jnp.float32)
    predicted = jnp.dot(features, reward_weight, preferred_element_type=jnp.float32)
    act_block = scores.shape[1]
    payoff = reward_level.astype(jnp.float32) * 0.25
    full_scores, full_pred = (
        lax.all_to_all(scores, "acts", split_axis=0, concat_axis=1, tiled=True),
        lax.all_to_all(predicted, "acts", split_axis=0, concat_axis=1, tiled=True),
    )
    part_rows = full_scores.shape[0]
    offset = lax.axis_index("acts") * part_rows
    my_action = lax.dynamic_slice_in_dim(logged_action, offset, part_rows)
    my_payoff = lax.dynamic_slice_in_dim(payoff, offset, part_rows)
    my_propensity = lax.dynamic_slice_in_dim(logged_propensity, offset, part_rows)
    all_columns = jnp.arange(full_scores.shape[1], dtype=jnp.int32)
    row_onehot = my_action[:, None] == all_columns[None, :]
    largest = jnp.max(full_scores, axis=1, keepdims=True)
    exponent = jnp.exp(full_scores - largest)
    row_total = jnp.sum(exponent, axis=1)
    weighted = jnp.sum(exponent * full_pred, axis=1)
    picked_exp = jnp.sum(jnp.where(row_onehot, exponent, jnp.float32(0.0)), axis=1)
    picked_pred = jnp.sum(jnp.where(row_onehot, full_pred, jnp.float32(0.0)), axis=1)
    rows_policy, rows_reward, rows_value = finish_rows(
        exponent,
        row_total,
        weighted,
        picked_exp,
        picked_pred,
        full_pred,
        row_onehot,
        my_payoff,
        my_propensity,
    )
    policy_term, reward_term = (
        lax.all_to_all(rows_policy, "acts", split_axis=1, concat_axis=0, tiled=True),
        lax.all_to_all(rows_reward, "acts", split_axis=1, concat_axis=0, tiled=True),
    )
    row_value = lax.all_gather(rows_value, "acts", axis=0, tiled=True)
    stacked = jnp.concatenate((policy_term, reward_term), axis=1)
    partial_grad = lax.dot_general(
        features, stacked, (((0,), (0,)), ((), ())), preferred_element_type=jnp.float32
    )
    summed = lax.psum(partial_grad.astype(jnp.bfloat16), "rows").astype(jnp.float32)
    return (summed[:, :act_block], summed[:, act_block:], row_value)


def solution(mesh):
    return jax.shard_map(
        on_device,
        mesh=mesh,
        in_specs=(
            P("rows", None),
            P(None, "acts"),
            P(None, "acts"),
            P("rows"),
            P("rows"),
            P("rows"),
        ),
        out_specs=(P(None, "acts"), P(None, "acts"), P("rows")),
        check_vma=False,
    )
```

profile of v0, /device:TPU:0, one launch (start us, length us, event | category | flops | bytes accessed | tf_op | source)
XLA Modules:
  0.0 741.3 jit_solution(5516784321706224198)
XLA Ops:
  7.2 1.6 copy-done
  8.8 14.4 %fusion.20 = f32[4096,512]{1,0:T(8,128)} fusion(bf16[4096,2048]{1,0:T(8,128)(2,1)} %param.6, bf16[2048,512]{1,0:T(8,128)(2,1)S(1)} %copy-done), kind=kOutput, calls=%fused_computation.31 | convolution fusion | flops 8589934592 | bytes 27262976 | tf_op jit(solution)/shard_map/dot_general | solution.py:28
  23.2 7.4 all-to-all-start
  30.5 14.4 %fusion.21 = f32[4096,512]{1,0:T(8,128)} fusion(bf16[4096,2048]{1,0:T(8,128)(2,1)} %param.6, bf16[2048,512]{1,0:T(8,128)(2,1)S(1)} %copy-done.2), kind=kOutput, calls=%fused_computation.32 | convolution fusion | flops 8589934592 | bytes 27262976 | tf_op jit(solution)/shard_map/dot_general | solution.py:29
  45.0 168.8 %all-to-all-done = f32[8,512,512]{2,1,0:T(8,128)} async-done(((f32[8,512,512]{2,1,0:T(8,128)}), f32[8,512,512]{2,1,0:T(8,128)}, u32[]{:S(2)}, u32[]{:S(2)}) %all-to-all-start) | async-done | bytes 8388640 | tf_op jit(solution)/shard_map/all_to_all | solution.py:33
  213.7 5.0 all-to-all-start.1
  218.8 0.2 all-reduce.2.cloned.1.call-start
  219.0 0.8 dynamic_slice.9
  219.8 3.8 reduce_max.9
  223.6 4.6 fusion.13
  228.2 172.7 %all-to-all-done.1 = f32[8,512,512]{2,1,0:T(8,128)} async-done(((f32[8,512,512]{2,1,0:T(8,128)}), f32[8,512,512]{2,1,0:T(8,128)}, u32[]{:S(2)}, u32[]{:S(2)}) %all-to-all-start.1) | async-done | bytes 8388640 | tf_op jit(solution)/shard_map/all_to_all | solution.py:34
  401.0 7.6 %fusion.11 = (f32[512]{0:T(512)S(1)}, f32[512]{0:T(512)S(1)}, f32[512]{0:T(512)S(1)}) fusion(f32[8,512,512]{2,1,0:T(8,128)} %all-to-all-done.1, f32[8,512,512]{2,1,0:T(8,128)} %all-to-all-done, f32[512]{0:T(512)S(1)} %reduce_max.9, s32[8,512]{1,0:T(8,128)S(1)} %multiply_add_fusion, s32[512]{0:T(512)S(1)} %dynamic_slice.9), kind=kLoop, calls=%fused_computation.18 | loop fusion | flops 16775680 | bytes 16803840 | tf_op jit(solution)/shard_map/reduce_sum | solution.py:46
  408.6 0.8 fusion.18
  409.4 8.0 %fusion.5 = (bf16[512,8,512]{2,0,1:T(8,128)(2,1)S(1)}, bf16[512,8,512]{2,0,1:T(8,128)(2,1)S(1)}) fusion(f32[8,512,512]{2,1,0:T(8,128)} %all-to-all-done.1, f32[8,512,512]{2,1,0:T(8,128)} %all-to-all-done, f32[512]{0:T(512)S(1)} %get-tuple-element.14, s32[8,512]{1,0:T(8,128)S(1)} %multiply_add_fusion, f32[512]{0:T(512)S(1)} %get-tuple-element.13, ...), kind=kLoop, calls=%fused_computation.9 | loop fusion | flops 27262976 | bytes 25194496 | tf_op jit(solution)/shard_map/convert_element_type | solution.py:18
  417.4 96.7 %all_to_all.61 = bf16[512,8,512]{2,0,1:T(8,128)(2,1)S(1)} all-to-all(bf16[512,8,512]{2,0,1:T(8,128)(2,1)S(1)} %get-tuple-element.15), channel_id=1, replica_groups=mesh['rows'=4,'acts'=8] {'acts'}, dimensions={1} | all-to-all | bytes 8388608 | tf_op jit(solution)/shard_map/all_to_all | solution.py:61
  514.1 96.5 %all_to_all.62 = bf16[512,8,512]{2,0,1:T(8,128)(2,1)S(1)} all-to-all(bf16[512,8,512]{2,0,1:T(8,128)(2,1)S(1)} %get-tuple-element.16), channel_id=1, replica_groups=mesh['rows'=4,'acts'=8] {'acts'}, dimensions={1} | all-to-all | bytes 8388608 | tf_op jit(solution)/shard_map/all_to_all | solution.py:62
  610.6 21.2 %convert_bitcast_fusion = bf16[2048,1024]{0,1:T(8,128)(2,1)} fusion(bf16[4096,2048]{1,0:T(8,128)(2,1)} %param.6, bf16[4096,512]{1,0:T(8,128)(2,1)S(1)} %bitcast.39, bf16[4096,512]{1,0:T(8,128)(2,1)S(1)} %bitcast.38), kind=kOutput, calls=%fused_computation.23 | convolution fusion | flops 17198743552 | bytes 29360128 | tf_op jit(solution)/shard_map/dot_general | solution.py:66
  631.8 0.0 all-reduce.2.cloned.1.call-update
  631.9 26.0 %all-gather = f32[8,1,512]{2,1,0:T(1,128)S(1)} all-gather(f32[1,1,512]{2,1,0:T(1,128)S(1)} %bitcast.41), channel_id=1, replica_groups=mesh['rows'=4,'acts'=8] {'acts'}, dimensions={0}, use_global_device_ids=true | all-gather | bytes 18432 | tf_op jit(solution)/shard_map/all_gather | solution.py:64
  657.9 58.4 %all-reduce.2.cloned.1.call-done = bf16[2048,1024]{0,1:T(8,128)(2,1)} async-done(((bf16[2048,1024]{0,1:T(8,128)(2,1)}), bf16[2048,1024]{0,1:T(8,128)(2,1)}) %all-reduce.2.cloned.1.call-update) | async-done | bytes 4194320 | tf_op jit(solution)/shard_map/psum | solution.py:69
  716.3 6.7 fusion.19
  723.0 5.5 copy.11
  728.5 5.3 copy.12
  733.8 0.6 copy.15
  (6 shorter events, 0.0 us)
Async XLA Ops:
  7.2 1.6 copy-start
  23.2 7.4 copy-start.2
  23.2 190.6 %all-to-all-start = ((f32[8,512,512]{2,1,0:T(8,128)}), f32[8,512,512]{2,1,0:T(8,128)}, u32[]{:S(2)}, u32[]{:S(2)}) async-start(f32[8,512,512]{2,1,0:T(8,128)} %bitcast.37), calls=%async_computation | async-start | bytes 16777216 | tf_op jit(solution)/shard_map/all_to_all | solution.py:33
  213.7 187.2 %all-to-all-start.1 = ((f32[8,512,512]{2,1,0:T(8,128)}), f32[8,512,512]{2,1,0:T(8,128)}, u32[]{:S(2)}, u32[]{:S(2)}) async-start(f32[8,512,512]{2,1,0:T(8,128)} %bitcast.36), calls=%async_computation.1 | async-start | bytes 16777216 | tf_op jit(solution)/shard_map/all_to_all | solution.py:34
  218.8 497.5 %all-reduce.2.cloned.1.call-start = ((), (), s32[]{:S(2)}) async-start(), calls=%async_computation.4 | async-start | bytes 8388608 | tf_op jit(solution)/shard_map/psum | solution.py:69
  723.0 11.4 %copy-start.1 = (bf16[2048,512]{1,0:T(8,128)(2,1)S(1)}, bf16[2048,512]{1,0:T(8,128)(2,1)}, u32[]{:S(2)}) copy-start(bf16[2048,512]{1,0:T(8,128)(2,1)} %param.7) | copy-start | bytes 6291460
Sparse Core Ops, SparseCore 0:
  632.0 84.2 all-reduce.1
where the time goes:
time: 742 us; the launch traced here: 741 us
  waiting for transfers between devices  400 us (54%)
  blocking collectives  219 us (30%)
  matrix products  50 us (7%)
  other arithmetic  24.9 us (3%)
  local copies, waits for them, and re-layouts  20.5 us (3%)
  between operations  14.1 us (2%)
  starting transfers between devices  12.6 us (2%)
    all_to_all x1, waiting for transfers between devices, on_device(): lax.all_to_all(predicted, 'acts', split_axis=0, concat_axis=1, tiled=True)  173 us
    all_to_all x1, waiting for transfers between devices, on_device(): lax.all_to_all(scores, 'acts', split_axis=0, concat_axis=1, tiled=True)  169 us
    all_to_all x1, blocking collectives, on_device(): lax.all_to_all(rows_policy, 'acts', split_axis=1, concat_axis=0, tiled=True)  96.7 us
    all_to_all x1, blocking collectives, on_device(): lax.all_to_all(rows_reward, 'acts', split_axis=1, concat_axis=0, tiled=True)  96.5 us
    psum x1, waiting for transfers between devices, on_device(): lax.psum(partial_grad.astype(jnp.bfloat16), 'rows').astype(jnp.float32)  58.4 us
    all_gather x1, blocking collectives, on_device(): row_value = lax.all_gather(rows_value, 'acts', axis=0, tiled=True)  26 us
    dot_general x1, matrix products, on_device(): lax.dot_general(features, stacked, (((0,), (0,)), ((), ())), preferred_el...  21.2 us
  transfers between devices with their start and end apart: 3, of which 3 were waited for; matrix products, arithmetic and copies ran while one was open for 3% of the time, Pallas kernels for 0%

commit v1 on v0

v1 whole, which is shorter than its diff:
```python
import jax
import jax.numpy as jnp
from jax import lax
from jax.sharding import PartitionSpec as P


def on_device(
    features, policy_weight, reward_weight, logged_action, reward_level, logged_propensity
):
    scores = jnp.dot(features, policy_weight, preferred_element_type=jnp.float32)
    predicted = jnp.dot(features, reward_weight, preferred_element_type=jnp.float32)
    act_block = scores.shape[1]
    payoff = reward_level.astype(jnp.float32) * 0.25
    columns = lax.axis_index("acts") * act_block + jnp.arange(act_block, dtype=jnp.int32)
    onehot = logged_action[:, None] == columns[None, :]
    local_max = jnp.max(scores, axis=1)
    exponent = jnp.exp(scores - local_max[:, None])
    zero = jnp.float32(0.0)
    stats = jnp.stack(
        (
            local_max,
            jnp.sum(exponent, axis=1),
            jnp.sum(exponent * predicted, axis=1),
            jnp.sum(jnp.where(onehot, exponent, zero), axis=1),
            jnp.sum(jnp.where(onehot, predicted, zero), axis=1),
        )
    )
    every = lax.all_gather(stats, "acts", axis=0)
    largest = jnp.max(every[:, 0], axis=0)
    rescale = jnp.exp(every[:, 0] - largest)
    row_total = jnp.sum(every[:, 1] * rescale, axis=0)
    mean_pred = jnp.sum(every[:, 2] * rescale, axis=0) / row_total
    picked_exp = jnp.sum(every[:, 3] * rescale, axis=0)
    picked_pred = jnp.sum(every[:, 4], axis=0)
    corrected = picked_exp / row_total / logged_propensity * (payoff - picked_pred)
    row_value = mean_pred + corrected
    probability = exponent * (jnp.exp(local_max - largest) / row_total)[:, None]
    policy_term = (
        probability * (predicted - mean_pred[:, None])
        + corrected[:, None] * (onehot.astype(jnp.float32) - probability)
    ).astype(jnp.bfloat16)
    reward_term = jnp.where(onehot, predicted - payoff[:, None], zero).astype(jnp.bfloat16)

    def grad_of(term):
        partial = lax.dot_general(
            features, term, (((0,), (0,)), ((), ())), preferred_element_type=jnp.float32
        )
        return lax.psum(partial.astype(jnp.bfloat16), "rows").astype(jnp.float32)

    reward_grad = grad_of(reward_term)
    return (grad_of(policy_term), reward_grad, row_value)


def solution(mesh):
    return jax.shard_map(
        on_device,
        mesh=mesh,
        in_specs=(
            P("rows", None),
            P(None, "acts"),
            P(None, "acts"),
            P("rows"),
            P("rows"),
            P("rows"),
        ),
        out_specs=(P(None, "acts"), P(None, "acts"), P("rows")),
        check_vma=False,
    )
```

time: 742 us -> 215 us (0.29)
  waiting for transfers between devices: 400 us -> 86.7 us
  blocking collectives: 219 us -> 34.8 us
  other arithmetic: 24.9 us -> 1.62 us
  matrix products: 50 us -> 68.9 us
  starting transfers between devices: 12.6 us -> 0.04 us
  local copies, waits for them, and re-layouts: 20.5 us -> 8.39 us
    all_to_all x2 -> x0, waiting for transfers between devices: 341 us -> none  [the longest x1 173 us: on_device(): lax.all_to_all(predicted, 'acts', split_axis=0, concat_axis=1, tiled=True)]
    all_to_all x2 -> x0, blocking collectives: 193 us -> none  [the longest x1 96.7 us: on_device(): lax.all_to_all(rows_policy, 'acts', split_axis=1, concat_axis=0, tiled=True)]
    psum x1, waiting for transfers between devices: 58.4 us -> 86.7 us  [grad_of(): return lax.psum(partial.astype(jnp.bfloat16), 'rows').astype(jnp.float32)]
    dot_general x1 -> x2, matrix products: 21.2 us -> 35.5 us  [grad_of(): lax.dot_general(features, term, (((0,), (0,)), ((), ())), preferred_eleme...]
    all_to_all x2 -> x0, starting transfers between devices: 12.4 us -> none  [the longest x1 7.39 us: on_device(): lax.all_to_all(scores, 'acts', split_axis=0, concat_axis=1, tiled=True)]
    reduce_sum x2 -> x1, other arithmetic: 12.2 us -> 0.43 us  [on_device(): mean_pred = jnp.sum(every[:, 2] * rescale, axis=0) / row_total]
    all_gather x1, blocking collectives: 26 us -> 34.8 us  [on_device(): every = lax.all_gather(stats, 'acts', axis=0)]
    convert_element_type x1 -> x0, other arithmetic: 8 us -> none  [finish_rows(): policy_term = (probability * (predicted - mean_pred[:, None]) + corrected...]
  transfers between devices with their start and end apart: 3 -> 1, of which waited for: 3 -> 1; matrix products, arithmetic and copies ran while one was open for 3% -> 0% of each run, Pallas kernels for 0% -> 0%
where the time goes in v1:
time: 215 us
  waiting for transfers between devices  86.7 us (40%)
  matrix products  68.9 us (32%)
  blocking collectives  34.8 us (16%)
  between operations  14.1 us (7%)
  local copies, waits for them, and re-layouts  8.39 us (4%)
    psum x1, waiting for transfers between devices, grad_of(): return lax.psum(partial.astype(jnp.bfloat16), 'rows').astype(jnp.float32)  86.7 us
    dot_general x2, matrix products, grad_of(): lax.dot_general(features, term, (((0,), (0,)), ((), ())), preferred_eleme...  35.5 us
    all_gather x1, blocking collectives, on_device(): every = lax.all_gather(stats, 'acts', axis=0)  34.8 us
    dot_general x1, matrix products, on_device(): jnp.dot(features, reward_weight, preferred_element_type=jnp.float32)  18 us
    dot_general x1, matrix products, on_device(): jnp.dot(features, policy_weight, preferred_element_type=jnp.float32)  15.3 us
    unnamed x10, local copies, waits for them, and re-layouts  8.27 us
  transfers between devices with their start and end apart: 1, of which 1 were waited for; matrix products, arithmetic and copies ran while one was open for 0% of the time, Pallas kernels for 0%

profile of v1, /device:TPU:0, one launch (start us, length us, event | category | flops | bytes accessed | tf_op | source)
XLA Modules:
  0.0 214.6 jit_solution(3191419998772855561)
XLA Ops:
  7.2 0.0 copy-start
  7.2 0.0 all-reduce.3.cloned.1.call-start
  7.2 0.0 copy-start.3
  7.3 15.3 %fusion.44 = (f32[4096]{0:T(1024)S(1)}, f32[4096,512]{0,1:T(8,128)}) fusion(bf16[4096,2048]{1,0:T(8,128)(2,1)} %param.6, bf16[2048,512]{1,0:T(8,128)(2,1)} %param.7), kind=kOutput, calls=%fused_computation.50 | convolution fusion | flops 8592027648 | bytes 27279360 | tf_op jit(solution)/shard_map/dot_general | solution.py:10
  22.6 0.0 copy-done
  22.6 0.0 copy-done.3
  22.6 0.0 copy-start.1
  22.6 0.0 copy-start.2
  22.6 18.0 %fusion = (f32[4096]{0:T(1024)S(1)}, f32[4096]{0:T(1024)S(1)}, f32[4096]{0:T(1024)S(1)}, f32[4096]{0:T(1024)S(1)}, f32[4096,512]{0,1:T(8,128)}) fusion(f32[4096,512]{0,1:T(8,128)} %get-tuple-element.32, s32[4096]{0:T(1024)S(1)} %copy-done.3, f32[4096]{0:T(1024)S(1)} %get-tuple-element.31, s32[512]{0:T(512)S(1)} %iota_add_fusion, ...), kind=kOutput, calls=%fused_computation.4 | convolution fusion | flops 8608792576 | bytes 35751936 | tf_op jit(solution)/shard_map/dot_general | solution.py:11
  40.6 0.1 stack.23
  40.8 34.8 %all-gather.1 = f32[8,5,4096]{2,1,0:T(8,128)S(1)} all-gather(f32[1,5,4096]{2,1,0:T(8,128)S(1)} %bitcast.44), channel_id=2, replica_groups=mesh['rows'=4,'acts'=8] {'acts'}, dimensions={0}, use_global_device_ids=true | all-gather | bytes 737280 | tf_op jit(solution)/shard_map/all_gather | solution.py:28
  75.6 0.6 fusion.43
  76.2 0.4 fusion.35
  76.6 0.0 copy-done.1
  76.6 0.0 copy-done.2
  76.6 0.6 fusion.42
  77.3 15.9 %fusion.31 = bf16[2048,512]{0,1:T(8,128)(2,1)} fusion(bf16[4096,2048]{1,0:T(8,128)(2,1)} %param.6, f32[4096,512]{0,1:T(8,128)} %get-tuple-element.33, f32[4096]{0:T(1024)S(1)} %get-tuple-element.29, s32[4096]{0:T(1024)S(1)} %copy-done.3, s32[512]{0:T(512)S(1)} %iota_add_fusion), kind=kOutput, calls=%fused_computation.29 | convolution fusion | flops 8599371776 | bytes 27297792 | tf_op jit(solution)/shard_map/dot_general | solution.py:45
  93.1 19.7 %fusion.28 = bf16[2048,512]{0,1:T(8,128)(2,1)} fusion(bf16[4096,2048]{1,0:T(8,128)(2,1)} %param.6, f32[4096,512]{0,1:T(8,128)} %get-tuple-element.33, f32[4096,512]{0,1:T(8,128)} %get-tuple-element.32, f32[4096]{0:T(1024)S(1)} %get-tuple-element.22, f32[4096]{0:T(1024)S(1)} %get-tuple-element.21, f32[4096]{0:T(1024)S(1)} %get-tuple-element.30, ...), kind=kOutput, calls=%fused_computation.28 | convolution fusion | flops 8611954688 | bytes 35735552 | tf_op jit(solution)/shard_map/dot_general | solution.py:45
  112.8 0.0 all-reduce.3.cloned.1.call-update
  112.8 86.7 %all-reduce.3.cloned.1.call-done = (bf16[2048,512]{0,1:T(8,128)(2,1)}, bf16[2048,512]{0,1:T(8,128)(2,1)}) async-done(((bf16[2048,512]{0,1:T(8,128)(2,1)}, bf16[2048,512]{0,1:T(8,128)(2,1)}), (bf16[2048,512]{0,1:T(8,128)(2,1)}, bf16[2048,512]{0,1:T(8,128)(2,1)})) %all-reduce.3.cloned.1.call-update) | async-done | bytes 4194320 | tf_op jit(solution)/shard_map/psum | solution.py:48
  199.5 4.1 %copy.17 = f32[2048,512]{1,0:T(8,128)} copy(bf16[2048,512]{0,1:T(8,128)(2,1)} %get-tuple-element.18) | data formatting | bytes 6291456
  203.6 4.1 %copy.18 = f32[2048,512]{1,0:T(8,128)} copy(bf16[2048,512]{0,1:T(8,128)(2,1)} %get-tuple-element.19) | data formatting | bytes 6291456
  (1 shorter events, 0.0 us)
Async XLA Ops:
  7.2 15.4 %copy-start = (bf16[2048,512]{1,0:T(8,128)(2,1)S(1)}, bf16[2048,512]{1,0:T(8,128)(2,1)}, u32[]{:S(2)}) copy-start(bf16[2048,512]{1,0:T(8,128)(2,1)} %param.8) | copy-start | bytes 6291460
  7.2 192.3 %all-reduce.3.cloned.1.call-start = ((), (), s32[]{:S(2)}) async-start(), calls=%async_computation | async-start | bytes 8388608 | tf_op jit(solution)/shard_map/psum | solution.py:48
  7.2 15.3 %copy-start.3 = (s32[4096]{0:T(1024)S(1)}, s32[4096]{0:T(1024)}, u32[]{:S(2)}) copy-start(s32[4096]{0:T(1024)} %param.9) | copy-start | bytes 49156
  22.6 54.0 %copy-start.1 = (s32[4096]{0:T(1024)S(1)}, s32[4096]{0:T(1024)}, u32[]{:S(2)}) copy-start(s32[4096]{0:T(1024)} %param.10) | copy-start | bytes 49156
  22.6 54.0 %copy-start.2 = (f32[4096]{0:T(1024)S(1)}, f32[4096]{0:T(1024)}, u32[]{:S(2)}) copy-start(f32[4096]{0:T(1024)} %param.11) | copy-start | bytes 49156
Sparse Core Ops, SparseCore 0:
  112.9 86.4 all-reduce.2

commit v2 on v1

v2 whole, which is shorter than its diff:
```python
import functools

import jax
import jax.numpy as jnp
from jax import lax
from jax.experimental import pallas as pl
from jax.experimental.pallas import tpu as pltpu
from jax.sharding import PartitionSpec as P

CORES = 2
F32 = jnp.float32
BF16 = jnp.bfloat16
MESH = pl.DeviceIdType.MESH


def kernel(
    n_rows,
    n_acts,
    dc,
    rc,
    feat_hbm,
    wp_hbm,
    wr_hbm,
    action_ref,
    level_ref,
    prop_ref,
    sums,
    value_ref,
    feat,
    w_raw,
    w_t,
    pred,
    expo,
    term,
    part,
    core_in,
    pair,
    st,
    st_in,
    fin,
    feat_sem,
    w_sem,
    core_send,
    core_recv,
    y_send,
    y_recv,
    own_send,
    own_recv,
    fwd_send,
    fwd_recv,
    loc_sem,
    st_send,
    st_recv,
    fin_send,
    fin_recv,
):
    rows, depth = feat.shape
    acts = pred.shape[0]
    half = acts // CORES
    n_y = n_rows // CORES
    my_row = lax.axis_index("rows")
    my_act = lax.axis_index("acts")
    my_y = my_row // CORES
    my_c = lax.rem(my_row, CORES)
    other_core = {"rows": my_y * CORES + 1 - my_c}
    own_at = pl.multiple_of(my_c * half, half)
    other_at = pl.multiple_of((1 - my_c) * half, half)
    n_d = depth // dc
    n_blocks = rows // rc
    rp = rows // n_acts

    def y_dev(j):
        return {"rows": lax.rem(my_y + j, n_y) * CORES + my_c}

    def act_dev(j):
        return {"acts": lax.rem(my_act + j, n_acts)}

    def feat_copy(b):
        at = pl.ds(pl.multiple_of(b * rc, rc), rc)
        return pltpu.make_async_copy(feat_hbm.at[at], feat.at[at], feat_sem.at[b])

    wr_copy = pltpu.make_async_copy(wr_hbm, w_raw.at[0], w_sem.at[0])
    wp_copy = pltpu.make_async_copy(wp_hbm, w_raw.at[1], w_sem.at[1])
    wr_copy.start()
    for b in range(n_blocks):
        feat_copy(b).start()
        if b == 0:
            wp_copy.start()

    barrier = pltpu.get_barrier_semaphore()
    peers = [other_core] + [y_dev(j) for j in range(1, n_y)] + [act_dev(j) for j in range(1, n_acts)]
    for peer in peers:
        pl.semaphore_signal(barrier, inc=1, device_id=peer, device_id_type=MESH)

    st[...] = jnp.zeros_like(st)

    def transpose_weight(i):
        @pl.loop(0, depth // 256)
        def _(b):
            at = pl.ds(pl.multiple_of(b * 256, 256), 256)
            w_t[i, :, at] = w_raw[i, at, :].T

    def block_at(b):
        return pl.ds(pl.multiple_of(b * rc, rc), rc)

    def times_features(i, at):
        return lax.dot_general(
            w_t[i], feat[at, :], (((1,), (1,)), ((), ())), preferred_element_type=F32
        )

    def chosen(at):
        mine = lax.broadcasted_iota(jnp.int32, (acts, rc), 0) + my_act * acts
        return mine == action_ref[:, at]

    wr_copy.wait()
    transpose_weight(0)

    @pl.loop(0, n_blocks)
    def _(b):
        at = block_at(b)
        feat_copy(b).wait()
        p = times_features(0, at)
        pred[:, at] = p
        onehot = chosen(at)
        payoff = level_ref[:, at].astype(F32) * 0.25
        st[4:5, at] = jnp.sum(jnp.where(onehot, p, 0.0), axis=0, keepdims=True)
        term[:, at] = jnp.where(onehot, p - payoff, 0.0).astype(BF16)

    pl.semaphore_wait(barrier, len(peers))

    def core_copy(k):
        return pltpu.make_async_remote_copy(
            src_ref=part.at[k, pl.ds(other_at, half)],
            dst_ref=core_in.at[k],
            send_sem=core_send.at[k],
            recv_sem=core_recv.at[k],
            device_id=other_core,
            device_id_type=MESH,
        )

    def pair_copy(k, device, send, recv):
        return pltpu.make_async_remote_copy(
            src_ref=pair.at[k],
            dst_ref=sums.at[my_y, k, pl.ds(own_at, half)],
            send_sem=send,
            recv_sem=recv,
            device_id=device,
            device_id_type=MESH,
        )

    def y_copy(k, j):
        return pair_copy(k, y_dev(j), y_send.at[k, j - 1], y_recv.at[k, j - 1])

    def own_copy(k):
        return pair_copy(k, other_core, own_send.at[k], own_recv.at[k])

    def loc_copy(k):
        return pltpu.make_async_copy(
            pair.at[k], sums.at[my_y, k, pl.ds(own_at, half)], loc_sem.at[k]
        )

    def fwd_copy(k, j):
        block = sums.at[lax.rem(my_y + n_y - j, n_y), k, pl.ds(own_at, half)]
        return pltpu.make_async_remote_copy(
            src_ref=block,
            dst_ref=block,
            send_sem=fwd_send.at[k, j - 1],
            recv_sem=fwd_recv.at[k, j - 1],
            device_id=other_core,
            device_id_type=MESH,
        )

    def pass_on(k):
        core_copy(k).wait_recv()
        own = part[k, pl.ds(own_at, half), :].astype(F32)
        pair[k] = (own + core_in[k].astype(F32)).astype(BF16)
        for j in range(1, n_y):
            y_copy(k, j).start()
        own_copy(k).start()
        loc_copy(k).start()

    def chunk(k):
        d_at = pl.ds(pl.multiple_of(lax.rem(k, n_d) * dc, dc), dc)
        part[k] = jnp.dot(term[...], feat[:, d_at], preferred_element_type=F32).astype(BF16)
        core_copy(k).start()

    def chunks(first, last):
        @pl.loop(first, last)
        def _(k):
            chunk(k)

            @pl.when(k > 0)
            def _():
                pass_on(k - 1)

    early = n_d // 4
    middle = (5 * n_d) // 8
    chunks(0, early)

    wp_copy.wait()
    transpose_weight(1)

    @pl.loop(0, n_blocks)
    def _(b):
        at = block_at(b)
        s = times_features(1, at)
        largest = jnp.max(s, axis=0, keepdims=True)
        e = jnp.exp(s - largest)
        expo[:, at] = e
        st[0:1, at] = largest
        st[1:2, at] = jnp.sum(e, axis=0, keepdims=True)
        st[2:3, at] = jnp.sum(e * pred[:, at], axis=0, keepdims=True)
        st[3:4, at] = jnp.sum(jnp.where(chosen(at), e, 0.0), axis=0, keepdims=True)

    def part_at(a):
        return pl.ds(pl.multiple_of(a * rp, rp), rp)

    def st_copy(j):
        return pltpu.make_async_remote_copy(
            src_ref=st.at[:, part_at(lax.rem(my_act + j, n_acts))],
            dst_ref=st_in.at[my_act],
            send_sem=st_send.at[j - 1],
            recv_sem=st_recv.at[j - 1],
            device_id=act_dev(j),
            device_id_type=MESH,
        )

    def fin_copy(j):
        return pltpu.make_async_remote_copy(
            src_ref=fin.at[:, part_at(my_act)],
            dst_ref=fin.at[:, part_at(my_act)],
            send_sem=fin_send.at[j - 1],
            recv_sem=fin_recv.at[j - 1],
            device_id=act_dev(j),
            device_id_type=MESH,
        )

    for j in range(1, n_acts):
        st_copy(j).start()
    st_in[my_act] = st[:, part_at(my_act)]

    chunks(early, middle)

    for j in range(1, n_acts):
        st_copy(j).wait_recv()
    mine = part_at(my_act)
    largest = st_in[0, 0:1, :]
    for a in range(1, n_acts):
        largest = jnp.maximum(largest, st_in[a, 0:1, :])
    row_total = jnp.zeros_like(largest)
    weighted = jnp.zeros_like(largest)
    picked_exp = jnp.zeros_like(largest)
    picked_pred = jnp.zeros_like(largest)
    for a in range(n_acts):
        rescale = jnp.exp(st_in[a, 0:1, :] - largest)
        row_total += st_in[a, 1:2, :] * rescale
        weighted += st_in[a, 2:3, :] * rescale
        picked_exp += st_in[a, 3:4, :] * rescale
        picked_pred += st_in[a, 4:5, :]
    mean_pred = weighted / row_total
    payoff = level_ref[:, mine].astype(F32) * 0.25
    corrected = picked_exp / row_total / prop_ref[:, mine] * (payoff - picked_pred)
    fin[:, mine] = jnp.concatenate(
        (largest, row_total, mean_pred, corrected) + (jnp.zeros_like(largest),) * 4, axis=0
    )
    for j in range(1, n_acts):
        fin_copy(j).start()

    chunks(middle, n_d)

    for j in range(1, n_acts):
        fin_copy(j).wait_recv()

    @pl.loop(0, n_blocks)
    def _(b):
        at = block_at(b)
        mean = fin[2:3, at]
        corr = fin[3:4, at]
        scale = jnp.exp(st[0:1, at] - fin[0:1, at]) / fin[1:2, at]
        probability = expo[:, at] * scale
        onehot = jnp.where(chosen(at), F32(1.0), F32(0.0))
        value_ref[:, at] = mean + corr
        term[:, at] = (
            probability * (pred[:, at] - mean) + corr * (onehot - probability)
        ).astype(BF16)

    chunks(n_d, 2 * n_d)
    pass_on(2 * n_d - 1)

    @pl.loop(0, 2 * n_d)
    def _(k):
        for j in range(1, n_y):
            y_copy(k, j).wait_recv()
            fwd_copy(k, j).start()

    @pl.loop(0, 2 * n_d)
    def _(k):
        core_copy(k).wait_send()
        own_copy(k).wait()
        loc_copy(k).wait()
        for j in range(1, n_y):
            y_copy(k, j).wait_send()
            fwd_copy(k, j).wait()

    for j in range(1, n_acts):
        st_copy(j).wait_send()
        fin_copy(j).wait_send()


def finish(reward_in, policy_in, value_in, policy_out, reward_out, value_out):
    for source, target in ((policy_in, policy_out), (reward_in, reward_out)):
        total = source[0, 0].astype(F32)
        for y in range(1, source.shape[0]):
            total += source[y, 0].astype(F32)
        target[...] = total.T
    value_out[...] = value_in[...]


def on_device(n_rows, n_acts, features, policy_weight, reward_weight, action, level, propensity):
    rows, depth = features.shape
    acts = policy_weight.shape[1]
    half = acts // CORES
    n_y = n_rows // CORES
    dc, rc = 256, 512
    n_d = depth // dc
    rp = rows // n_acts
    dma = pltpu.SemaphoreType.DMA
    others = max(n_y - 1, 1)
    sums, value = pl.pallas_call(
        functools.partial(kernel, n_rows, n_acts, dc, rc),
        out_shape=(
            jax.ShapeDtypeStruct((n_y, 2 * n_d, acts, dc), BF16),
            jax.ShapeDtypeStruct((1, rows), F32),
        ),
        in_specs=[pl.BlockSpec(memory_space=pl.ANY)] * 3
        + [pl.BlockSpec(memory_space=pltpu.VMEM)] * 3,
        out_specs=(
            pl.BlockSpec(memory_space=pl.ANY),
            pl.BlockSpec(memory_space=pltpu.VMEM),
        ),
        scratch_shapes=[
            pltpu.VMEM((rows, depth), BF16),
            pltpu.VMEM((2, depth, acts), BF16),
            pltpu.VMEM((2, acts, depth), BF16),
            pltpu.VMEM((acts, rows), F32),
            pltpu.VMEM((acts, rows), F32),
            pltpu.VMEM((acts, rows), BF16),
            pltpu.VMEM((2 * n_d, acts, dc), BF16),
            pltpu.VMEM((2 * n_d, half, dc), BF16),
            pltpu.VMEM((2 * n_d, half, dc), BF16),
            pltpu.VMEM((8, rows), F32),
            pltpu.VMEM((n_acts, 8, rp), F32),
            pltpu.VMEM((8, rows), F32),
            dma((rows // rc,)),
            dma((2,)),
            dma((2 * n_d,)),
            dma((2 * n_d,)),
            dma((2 * n_d, others)),
            dma((2 * n_d, others)),
            dma((2 * n_d,)),
            dma((2 * n_d,)),
            dma((2 * n_d, others)),
            dma((2 * n_d, others)),
            dma((2 * n_d,)),
            dma((n_acts - 1,)),
            dma((n_acts - 1,)),
            dma((n_acts - 1,)),
            dma((n_acts - 1,)),
        ],
        compiler_params=pltpu.CompilerParams(
            collective_id=0, has_side_effects=True, vmem_limit_bytes=62 * 1024 * 1024
        ),
        cost_estimate=pl.CostEstimate(
            flops=8 * rows * depth * acts,
            bytes_accessed=2 * rows * depth + 16 * depth * acts,
            transcendentals=rows * acts,
        ),
    )(
        features,
        policy_weight,
        reward_weight,
        action.reshape(1, rows),
        level.reshape(1, rows),
        propensity.reshape(1, rows),
    )
    grad_spec = pl.BlockSpec((dc, acts), lambda i: (i, 0))
    policy_grad, reward_grad, row_value = pl.pallas_call(
        finish,
        grid=(n_d,),
        out_shape=(
            jax.ShapeDtypeStruct((depth, acts), F32),
            jax.ShapeDtypeStruct((depth, acts), F32),
            jax.ShapeDtypeStruct((1, rows), F32),
        ),
        in_specs=[
            pl.BlockSpec((n_y, 1, acts, dc), lambda i: (0, i, 0, 0)),
            pl.BlockSpec((n_y, 1, acts, dc), lambda i: (0, i + n_d, 0, 0)),
            pl.BlockSpec((1, rows), lambda i: (0, 0)),
        ],
        out_specs=(grad_spec, grad_spec, pl.BlockSpec((1, rows), lambda i: (0, 0))),
        compiler_params=pltpu.CompilerParams(vmem_limit_bytes=32 * 1024 * 1024),
    )(sums, sums, value)
    return policy_grad, reward_grad, row_value.reshape(rows)


def solution(mesh):
    return jax.shard_map(
        functools.partial(on_device, mesh.shape["rows"], mesh.shape["acts"]),
        mesh=mesh,
        in_specs=(
            P("rows", None),
            P(None, "acts"),
            P(None, "acts"),
            P("rows"),
            P("rows"),
            P("rows"),
        ),
        out_specs=(P(None, "acts"), P(None, "acts"), P("rows")),
        check_vma=False,
    )
```

time: 215 us -> 97.2 us (0.45)
  Pallas kernels: 0 us -> 92.1 us
  waiting for transfers between devices: 86.7 us -> 0 us
  matrix products: 68.9 us -> 0 us
  blocking collectives: 34.8 us -> 0 us
  between operations: 14.1 us -> 0.65 us
  local copies, waits for them, and re-layouts: 8.39 us -> 4.09 us
    pallas_call x0 -> x2, Pallas kernels: none -> 92.1 us  [the longest x1 86.7 us: on_device(): pl.pallas_call(functools.partial(kernel, n_rows, n_acts, dc, rc), out_sha...]
    psum x1 -> x0, waiting for transfers between devices: 86.7 us -> none  [grad_of(): return lax.psum(partial.astype(jnp.bfloat16), 'rows').astype(jnp.float32)]
    dot_general x4 -> x0, matrix products: 68.9 us -> none  [the longest x2 35.5 us: grad_of(): lax.dot_general(features, term, (((0,), (0,)), ((), ())), preferred_eleme...]
    all_gather x1 -> x0, blocking collectives: 34.8 us -> none  [on_device(): every = lax.all_gather(stats, 'acts', axis=0)]
    unnamed x10 -> x4, local copies, waits for them, and re-layouts: 8.27 us -> 4.09 us
  transfers between devices with their start and end apart: 1 -> 0, of which waited for: 1 -> 0; matrix products, arithmetic and copies ran while one was open for 0% -> 0% of each run, Pallas kernels for 0% -> 0%
where the time goes in v2:
time: 97.2 us; the launch traced here: 96.8 us
  Pallas kernels  92.1 us (95%)
  local copies, waits for them, and re-layouts  4.09 us (4%)
    pallas_call x1, Pallas kernels, on_device(): pl.pallas_call(functools.partial(kernel, n_rows, n_acts, dc, rc), out_sha...  86.7 us
    pallas_call x1, Pallas kernels, on_device(): pl.pallas_call(finish, grid=(n_d,), out_shape=(jax.ShapeDtypeStruct((dept...  5.37 us
    unnamed x4, local copies, waits for them, and re-layouts  4.09 us

profile of v2, /device:TPU:0, one launch (start us, length us, event | category | flops | bytes accessed | tf_op | source)
XLA Modules:
  0.0 96.8 jit_solution(2285608810817349224)
XLA Ops:
  0.6 86.7 %shard_map.85 = (bf16[2,16,512,256]{3,2,1,0:T(8,128)(2,1)}, f32[1,4096]{1,0:T(1,128)}) custom-call(bf16[4096,2048]{1,0:T(8,128)(2,1)} %feat_hbm.1, bf16[2048,512]{1,0:T(8,128)(2,1)} %wp_hbm.1, bf16[2048,512]{1,0:T(8,128)(2,1)} %wr_hbm.1, s32[1,4096]{1,0:T(1,128)} %bitcast.4, s32[1,4096]{1,0:T(1,128)} %bitcast.5, f32[1,4096]{1,0:T(1,128)} %bitcast.6), custom_call_target="tpu_custom_call" | custom-call | flops 34359738368 | bytes 33554432 | tf_op jit(solution)/shard_map/pallas_call | solution.py:329
  87.3 0.0 copy-start
  87.3 3.4 %copy-done = bf16[2,16,512,256]{3,2,1,0:T(8,128)(2,1)S(1)} copy-done((bf16[2,16,512,256]{3,2,1,0:T(8,128)(2,1)S(1)}, bf16[2,16,512,256]{3,2,1,0:T(8,128)(2,1)}, u32[]{:S(2)}) %copy-start) | copy-done | bytes 8388632
  90.7 0.0 copy-start.1
  90.7 0.7 copy-done.1
  91.4 5.4 %shard_map.86 = (f32[2048,512]{1,0:T(8,128)}, f32[2048,512]{1,0:T(8,128)}, f32[1,4096]{1,0:T(1,128)}) custom-call(bf16[2,16,512,256]{3,2,1,0:T(8,128)(2,1)S(1)} %copy-done, bf16[2,16,512,256]{3,2,1,0:T(8,128)(2,1)S(1)} %copy-done, f32[1,4096]{1,0:T(1,128)S(1)} %copy-done.1), custom_call_target="tpu_custom_call" | custom-call | tf_op jit(solution)/shard_map/pallas_call | solution.py:387
Async XLA Ops:
  87.3 3.4 %copy-start = (bf16[2,16,512,256]{3,2,1,0:T(8,128)(2,1)S(1)}, bf16[2,16,512,256]{3,2,1,0:T(8,128)(2,1)}, u32[]{:S(2)}) copy-start(bf16[2,16,512,256]{3,2,1,0:T(8,128)(2,1)} %get-tuple-element.8.reward_in.policy_in) | copy-start | bytes 25165828
  90.7 0.7 copy-start.1

commit v3 on v2

--- a/solution.py
+++ b/solution.py
@@ -32,6 +32,7 @@
     pred,
     expo,
     term,
+    late_term,
     part,
     core_in,
     pair,
@@ -79,13 +80,11 @@
         at = pl.ds(pl.multiple_of(b * rc, rc), rc)
         return pltpu.make_async_copy(feat_hbm.at[at], feat.at[at], feat_sem.at[b])
 
-    wr_copy = pltpu.make_async_copy(wr_hbm, w_raw.at[0], w_sem.at[0])
-    wp_copy = pltpu.make_async_copy(wp_hbm, w_raw.at[1], w_sem.at[1])
+    wr_copy = pltpu.make_async_copy(wr_hbm, w_raw, w_sem.at[0])
+    wp_copy = pltpu.make_async_copy(wp_hbm, w_raw, w_sem.at[1])
     wr_copy.start()
     for b in range(n_blocks):
         feat_copy(b).start()
-        if b == 0:
-            wp_copy.start()
 
     barrier = pltpu.get_barrier_semaphore()
     peers = [other_core] + [y_dev(j) for j in range(1, n_y)] + [act_dev(j) for j in range(1, n_acts)]
@@ -98,7 +97,7 @@
         @pl.loop(0, depth // 256)
         def _(b):
             at = pl.ds(pl.multiple_of(b * 256, 256), 256)
-            w_t[i, :, at] = w_raw[i, at, :].T
+            w_t[i, :, at] = w_raw[at, :].T
 
     def block_at(b):
         return pl.ds(pl.multiple_of(b * rc, rc), rc)
@@ -114,17 +113,30 @@
 
     wr_copy.wait()
     transpose_weight(0)
-
-    @pl.loop(0, n_blocks)
-    def _(b):
+    wp_copy.start()
+
+    def predict(b):
         at = block_at(b)
-        feat_copy(b).wait()
-        p = times_features(0, at)
-        pred[:, at] = p
+        pred[:, at] = times_features(0, at)
+
+    def reward_terms(b):
+        at = block_at(b)
+        p = pred[:, at]
         onehot = chosen(at)
         payoff = level_ref[:, at].astype(F32) * 0.25
         st[4:5, at] = jnp.sum(jnp.where(onehot, p, 0.0), axis=0, keepdims=True)
         term[:, at] = jnp.where(onehot, p - payoff, 0.0).astype(BF16)
+
+    feat_copy(0).wait()
+    predict(0)
+
+    @pl.loop(1, n_blocks)
+    def _(b):
+        feat_copy(b).wait()
+        reward_terms(b - 1)
+        predict(b)
+
+    reward_terms(n_blocks - 1)
 
     pl.semaphore_wait(barrier, len(peers))
 
@@ -179,31 +191,37 @@
         own_copy(k).start()
         loc_copy(k).start()
 
-    def chunk(k):
+    def chunk(k, source):
         d_at = pl.ds(pl.multiple_of(lax.rem(k, n_d) * dc, dc), dc)
-        part[k] = jnp.dot(term[...], feat[:, d_at], preferred_element_type=F32).astype(BF16)
+        part[k] = jnp.dot(source[...], feat[:, d_at], preferred_element_type=F32).astype(BF16)
         core_copy(k).start()
 
-    def chunks(first, last):
+    def chunks(first, last, source, beside=None):
         @pl.loop(first, last)
         def _(k):
-            chunk(k)
+            if beside is not None:
+                beside(k - first)
+            chunk(k, source)
 
             @pl.when(k > 0)
             def _():
                 pass_on(k - 1)
 
     early = n_d // 4
-    middle = (5 * n_d) // 8
-    chunks(0, early)
+    middle = n_d // 2
+    late = (3 * n_d) // 4
+    chunks(0, early, term)
 
     wp_copy.wait()
     transpose_weight(1)
 
-    @pl.loop(0, n_blocks)
-    def _(b):
+    def score(b):
         at = block_at(b)
-        s = times_features(1, at)
+        expo[:, at] = times_features(1, at)
+
+    def exponents(b):
+        at = block_at(b)
+        s = expo[:, at]
         largest = jnp.max(s, axis=0, keepdims=True)
         e = jnp.exp(s - largest)
         expo[:, at] = e
@@ -211,6 +229,15 @@
         st[1:2, at] = jnp.sum(e, axis=0, keepdims=True)
         st[2:3, at] = jnp.sum(e * pred[:, at], axis=0, keepdims=True)
         st[3:4, at] = jnp.sum(jnp.where(chosen(at), e, 0.0), axis=0, keepdims=True)
+
+    score(0)
+
+    @pl.loop(1, n_blocks)
+    def _(b):
+        exponents(b - 1)
+        score(b)
+
+    exponents(n_blocks - 1)
 
     def part_at(a):
         return pl.ds(pl.multiple_of(a * rp, rp), rp)
@@ -239,7 +266,7 @@
         st_copy(j).start()
     st_in[my_act] = st[:, part_at(my_act)]
 
-    chunks(early, middle)
+    chunks(early, middle, term)
 
     for j in range(1, n_acts):
         st_copy(j).wait_recv()
@@ -266,13 +293,12 @@
     for j in range(1, n_acts):
         fin_copy(j).start()
 
-    chunks(middle, n_d)
+    chunks(middle, late, term)
 
     for j in range(1, n_acts):
         fin_copy(j).wait_recv()
 
-    @pl.loop(0, n_blocks)
-    def _(b):
+    def policy_terms(b):
         at = block_at(b)
         mean = fin[2:3, at]
         corr = fin[3:4, at]
@@ -280,11 +306,18 @@
         probability = expo[:, at] * scale
         onehot = jnp.where(chosen(at), F32(1.0), F32(0.0))
         value_ref[:, at] = mean + corr
-        term[:, at] = (
+        late_term[:, at] = (
             probability * (pred[:, at] - mean) + corr * (onehot - probability)
         ).astype(BF16)
 
-    chunks(n_d, 2 * n_d)
+    share = n_blocks // (n_d - late)
+
+    def policy_share(i):
+        for b in range(share):
+            policy_terms(i * share + b)
+
+    chunks(late, n_d, term, policy_share)
+    chunks(n_d, 2 * n_d, late_term)
     pass_on(2 * n_d - 1)
 
     @pl.loop(0, 2 * n_d)
@@ -340,10 +373,11 @@
         ),
         scratch_shapes=[
             pltpu.VMEM((rows, depth), BF16),
-            pltpu.VMEM((2, depth, acts), BF16),
+            pltpu.VMEM((depth, acts), BF16),
             pltpu.VMEM((2, acts, depth), BF16),
             pltpu.VMEM((acts, rows), F32),
             pltpu.VMEM((acts, rows), F32),
+            pltpu.VMEM((acts, rows), BF16),
             pltpu.VMEM((acts, rows), BF16),
             pltpu.VMEM((2 * n_d, acts, dc), BF16),
             pltpu.VMEM((2 * n_d, half, dc), BF16),
@@ -398,7 +432,7 @@
             pl.BlockSpec((1, rows), lambda i: (0, 0)),
         ],
         out_specs=(grad_spec, grad_spec, pl.BlockSpec((1, rows), lambda i: (0, 0))),
-        compiler_params=pltpu.CompilerParams(vmem_limit_bytes=32 * 1024 * 1024),
+        compiler_params=pltpu.CompilerParams(vmem_limit_bytes=62 * 1024 * 1024),
     )(sums, sums, value)
     return policy_grad, reward_grad, row_value.reshape(rows)
 

time: 97.2 us -> 99.8 us (1.027)
  Pallas kernels: 92.1 us -> 98.8 us
  local copies, waits for them, and re-layouts: 4.09 us -> 0 us
    unnamed x4 -> x0, local copies, waits for them, and re-layouts: 4.09 us -> none
    pallas_call x1, Pallas kernels: 5.37 us -> 9.28 us  [on_device(): pl.pallas_call(finish, grid=(n_d,), out_shape=(jax.ShapeDtypeStruct((dept...]
    pallas_call x1, Pallas kernels: 86.7 us -> 89.5 us  [on_device(): pl.pallas_call(functools.partial(kernel, n_rows, n_acts, dc, rc), out_sha...]
where the time goes in v3:
time: 99.8 us; the launch traced here: 99.4 us
  Pallas kernels  98.8 us (99%)
    pallas_call x1, Pallas kernels, on_device(): pl.pallas_call(functools.partial(kernel, n_rows, n_acts, dc, rc), out_sha...  89.5 us
    pallas_call x1, Pallas kernels, on_device(): pl.pallas_call(finish, grid=(n_d,), out_shape=(jax.ShapeDtypeStruct((dept...  9.28 us

profile of v3, /device:TPU:0, one launch (start us, length us, event | category | flops | bytes accessed | tf_op | source)
XLA Modules:
  0.0 99.4 jit_solution(1595131624562389232)
XLA Ops:
  0.6 89.5 %shard_map.85 = (bf16[2,16,512,256]{3,2,1,0:T(8,128)(2,1)}, f32[1,4096]{1,0:T(1,128)}) custom-call(bf16[4096,2048]{1,0:T(8,128)(2,1)} %feat_hbm.1, bf16[2048,512]{1,0:T(8,128)(2,1)} %wp_hbm.1, bf16[2048,512]{1,0:T(8,128)(2,1)} %wr_hbm.1, s32[1,4096]{1,0:T(1,128)} %bitcast.4, s32[1,4096]{1,0:T(1,128)} %bitcast.5, f32[1,4096]{1,0:T(1,128)} %bitcast.6), custom_call_target="tpu_custom_call" | custom-call | flops 34359738368 | bytes 33554432 | tf_op jit(solution)/shard_map/pallas_call | solution.py:362
  90.1 9.3 %shard_map.86 = (f32[2048,512]{1,0:T(8,128)}, f32[2048,512]{1,0:T(8,128)}, f32[1,4096]{1,0:T(1,128)}) custom-call(bf16[2,16,512,256]{3,2,1,0:T(8,128)(2,1)} %get-tuple-element.8.reward_in.policy_in, bf16[2,16,512,256]{3,2,1,0:T(8,128)(2,1)} %get-tuple-element.8.reward_in.policy_in, f32[1,4096]{1,0:T(1,128)} %get-tuple-element.9.value_in), custom_call_target="tpu_custom_call" | custom-call | tf_op jit(solution)/shard_map/pallas_call | solution.py:421
